TPU v7x, 32 devices: a whole 2x2x4 slice. The times are simulated.
32 devices in a mesh: rep: 2 (over y), dp: 2 (over core), tp: 8 (over z, x).
Axes of the slice: x: 2, y: 2, z: 4, core: 2. Of those that a mesh axis runs over, the one named last changes fastest.
Arguments:
- tokens: bfloat16 [16, 8192], P(('rep', 'dp')), parts along dimension 0, may hold values from -6 to 6
- gain: bfloat16 [8192], replicated, may hold values from 0.099609375 to 1.8984375
- query_matrix: bfloat16 [8192, 8192], P(None, 'tp'), may hold values from -0.0625 to 0.0625
- key_value_weight: bfloat16 [8192, 2048], P('tp'), may hold values from -0.0625 to 0.0625
- output_weight: bfloat16 [8192, 8192], P('tp'), may hold values from -0.5 to 0.5
- adapter_down_factors: bfloat16 [16, 48, 8192], P(('dp', 'tp')), may hold values from -0.0625 to 0.0625
- adapter_up_query: bfloat16 [16, 16, 8192], P(('dp', 'tp')), may hold values from -1.5 to 1.5
- adapter_up_key_value: bfloat16 [16, 2, 16, 1024], P(('dp', 'tp')), may hold values from -1.5 to 1.5
- tenant_slot_table: int32 [16], replicated, may hold values from 0 to 15, each once
- request_tenant_index: int32 [16], P('rep'), parts along dimension 0, may hold values from 0 to 15, as said below
- lengths: int32 [4, 4], P(('rep', 'dp')), parts along dimension 0, may hold values from 1 to 4096, 8192 in all within a row
- cache: bfloat16 [16, 32768, 256], P(('rep', 'dp'), 'tp'), parts along dimension 0, may hold values from -2000 to 2000
Outputs:
- mixed: bfloat16 [16, 8192], P(('rep', 'dp'), 'tp'), parts along dimension 0
There are 2 independent parts, one for each index of `rep`. A program takes and returns all parts, laid end to end along the dimension named above; an argument that names none is the same for every part. Nothing has to cross between parts.
Inputs may be any that keep to these rules, and one draw needn't show every extreme that they name: `request_tenant_index`: in each subgroup of 4 requests one tenant is named by exactly 2 requests and every other tenant by at most one.
All inputs are finite; a program needn't handle non-finite values.
Results may differ from a plain program's by a relative error of at most 0.0095.
The roundings to bfloat16 on the way count: a program that leaves them out, or rounds other values in their place, can miss the bound.
Values may be sent and summed in bfloat16 or wider, within the bound.
A program may use at most 128 MiB of HBM per device.

v0:
```python
import jax
import jax.numpy as jnp
from jax import lax
from jax.sharding import PartitionSpec as P

QUERY_HEADS = 64
KEY_VALUE_HEADS = 8
HEAD_SIZE = 128
ADAPTER_RANK = 16


theta_base = 500000.0
norm_eps = 1e-05
neutral = -1e30


def combined_all(part, axis, combine):
    gathered = jax.tree.map(lambda a: lax.all_gather(a, axis), part)

    def take(source):
        return jax.tree.map(lambda a: lax.dynamic_index_in_dim(a, source, 0, False), gathered)

    return lax.fori_loop(
        1, lax.axis_size(axis), lambda source, state: combine(state, take(source)), take(0)
    )


def rotate(vector, position):
    half_dim = vector.shape[-1] // 2
    frequency = jnp.power(
        jnp.float32(theta_base), -jnp.arange(half_dim, dtype=jnp.float32) * 2.0 / vector.shape[-1]
    )
    angles = position.astype(jnp.float32)[..., None] * frequency
    cos_table = jnp.cos(angles)
    sin_table = jnp.sin(angles)
    leading = vector[..., :half_dim]
    trailing = vector[..., half_dim:]
    return jnp.concatenate(
        [leading * cos_table - trailing * sin_table, trailing * cos_table + leading * sin_table],
        axis=-1,
    )


def slot_lookup(ids, tenant_slot_table):
    table = jnp.arange(tenant_slot_table.shape[0], dtype=jnp.int32)
    return jnp.sum(jnp.where(ids[:, None] == table[None, :], tenant_slot_table[None, :], 0), axis=1)


def combine_parts(earlier, later):
    top_early, total_early, acc_early = earlier
    top_late, total_late, acc_late = later
    highest = jnp.maximum(top_early, top_late)
    factor_early = jnp.exp(top_early - highest)
    factor_late = jnp.exp(top_late - highest)
    return (
        highest,
        total_early * factor_early + total_late * factor_late,
        acc_early * factor_early[..., None] + acc_late * factor_late[..., None],
    )


def on_device(
    tokens,
    gain,
    query_matrix,
    key_value_weight,
    output_weight,
    adapter_down_factors,
    adapter_up_query,
    adapter_up_key_value,
    tenant_slot_table,
    request_tenant_index,
    lengths,
    cache,
):
    tp_size = lax.axis_size("tp")
    dp_size = lax.axis_size("dp")
    tp_index = lax.axis_index("tp")
    dp_index = lax.axis_index("dp")
    requests = tokens.shape[0]
    per_dev = key_value_weight.shape[0]
    head_cols = query_matrix.shape[1]
    heads_here = head_cols // HEAD_SIZE
    group_size = QUERY_HEADS // KEY_VALUE_HEADS
    kv_span = tp_size // KEY_VALUE_HEADS
    kv_head = tp_index // kv_span
    span_pos = cache.shape[1] // KEY_VALUE_HEADS
    factor = HEAD_SIZE ** (-0.5)
    widened = tokens.astype(jnp.float32)
    inverse_rms = lax.rsqrt(jnp.mean(widened * widened, axis=1, keepdims=True) + norm_eps)
    normed = (widened * inverse_rms * gain.astype(jnp.float32)).astype(jnp.bfloat16)
    own_cols = lax.dynamic_slice_in_dim(normed, tp_index * per_dev, per_dev, 1)
    kv_part = jnp.dot(own_cols, key_value_weight, preferred_element_type=jnp.float32)
    device = dp_index * tp_size + tp_index
    request_index = lax.all_gather(normed, "dp", axis=0, tiled=True)
    all_slots = slot_lookup(request_tenant_index, tenant_slot_table)
    full_rank = lax.dot_general(
        request_index,
        adapter_down_factors[0],
        (((1,), (1,)), ((), ())),
        preferred_element_type=jnp.float32,
    )
    slot_rank_rows = jnp.where((all_slots == device)[:, None], full_rank, 0.0).astype(jnp.bfloat16)
    query_update = jnp.dot(
        slot_rank_rows[:, :ADAPTER_RANK], adapter_up_query[0], preferred_element_type=jnp.float32
    )
    delta_k = jnp.dot(
        slot_rank_rows[:, ADAPTER_RANK : 2 * ADAPTER_RANK],
        adapter_up_key_value[0, 0],
        preferred_element_type=jnp.float32,
    )
    delta_v = jnp.dot(
        slot_rank_rows[:, 2 * ADAPTER_RANK :],
        adapter_up_key_value[0, 1],
        preferred_element_type=jnp.float32,
    )
    q_blocks = query_update.reshape(dp_size, requests, tp_size, head_cols).transpose(0, 2, 1, 3)
    k_blocks = jnp.repeat(
        delta_k.reshape(dp_size, requests, KEY_VALUE_HEADS, HEAD_SIZE), kv_span, axis=2
    ).transpose(0, 2, 1, 3)
    v_blocks = jnp.repeat(
        delta_v.reshape(dp_size, requests, KEY_VALUE_HEADS, HEAD_SIZE), kv_span, axis=2
    ).transpose(0, 2, 1, 3)
    term = jnp.concatenate([q_blocks, k_blocks, v_blocks], axis=3).reshape(
        dp_size * tp_size, requests, head_cols + 2 * HEAD_SIZE
    )
    received = lax.psum_scatter(term, ("dp", "tp"), scatter_dimension=0, tiled=True)[0]
    kv_sum = lax.psum(kv_part, "tp")
    query_delta = received[:, :head_cols]
    key_delta = received[:, head_cols : head_cols + HEAD_SIZE]
    value_delta = received[:, head_cols + HEAD_SIZE :]
    query_raw = jnp.dot(normed, query_matrix, preferred_element_type=jnp.float32) + query_delta
    key_base = lax.dynamic_slice_in_dim(kv_sum, kv_head * HEAD_SIZE, HEAD_SIZE, 1)
    value_base = lax.dynamic_slice_in_dim(
        kv_sum, KEY_VALUE_HEADS * HEAD_SIZE + kv_head * HEAD_SIZE, HEAD_SIZE, 1
    )
    key_raw = key_base + key_delta
    value_raw = value_base + value_delta
    positions = lengths[0]
    query = rotate(query_raw.reshape(requests, heads_here, HEAD_SIZE), positions[:, None]).astype(
        jnp.bfloat16
    )
    key_new = rotate(key_raw, positions).astype(jnp.bfloat16)
    value_new = value_raw.astype(jnp.bfloat16)
    all_queries = lax.all_gather(query.reshape(requests, head_cols), "tp", axis=1, tiled=True)
    grouped = all_queries.reshape(requests, KEY_VALUE_HEADS, group_size, HEAD_SIZE)
    local_rows = cache.reshape(requests, span_pos, KEY_VALUE_HEADS, 2 * HEAD_SIZE)
    cached_keys = local_rows[..., :HEAD_SIZE]
    cached_values = local_rows[..., HEAD_SIZE:]
    scores = (
        jnp.einsum("rkgd,rpkd->rkgp", grouped, cached_keys, preferred_element_type=jnp.float32)
        * factor
    )
    slot_positions = tp_index * span_pos + jnp.arange(span_pos, dtype=jnp.int32)
    usable = (slot_positions[None, :] < positions[:, None])[:, None, None, :]
    scores = jnp.where(usable, scores, neutral)
    local_top = jnp.max(scores, axis=3)
    weights = jnp.where(usable, jnp.exp(scores - local_top[..., None]), 0.0)
    local_total = jnp.sum(weights, axis=3)
    local_acc = jnp.einsum("rkgp,rpkd->rkgd", weights, cached_values.astype(jnp.float32))
    local_top = local_top.reshape(requests, QUERY_HEADS)
    local_total = local_total.reshape(requests, QUERY_HEADS)
    local_acc = local_acc.reshape(requests, QUERY_HEADS, HEAD_SIZE)
    merged_top, merged_total, merged_acc = combined_all(
        (local_top, local_total, local_acc), "tp", combine_parts
    )
    first_head = tp_index * heads_here
    merged_top = lax.dynamic_slice_in_dim(merged_top, first_head, heads_here, 1)
    merged_total = lax.dynamic_slice_in_dim(merged_total, first_head, heads_here, 1)
    merged_acc = lax.dynamic_slice_in_dim(merged_acc, first_head, heads_here, 1)
    own_score = (
        jnp.einsum("rhd,rd->rh", query, key_new, preferred_element_type=jnp.float32) * factor
    )
    highest = jnp.maximum(merged_top, own_score)
    old_factor = jnp.exp(merged_top - highest)
    new_factor = jnp.exp(own_score - highest)
    totals = merged_total * old_factor + new_factor
    combined = (
        merged_acc * old_factor[..., None]
        + new_factor[..., None] * value_new.astype(jnp.float32)[:, None, :]
    )
    attended = (combined / totals[..., None]).reshape(requests, head_cols).astype(jnp.bfloat16)
    shares = lax.psum_scatter(
        lax.dot_general(
            output_weight, attended, (((0,), (1,)), ((), ())), preferred_element_type=jnp.float32
        ),
        "tp",
        scatter_dimension=0,
        tiled=True,
    )
    return shares.T.astype(jnp.bfloat16)


def solution(mesh):
    in_specs = (
        P(("rep", "dp"), None),
        P(),
        P(None, "tp"),
        P("tp", None),
        P("tp", None),
        P(("dp", "tp"), None, None),
        P(("dp", "tp"), None, None),
        P(("dp", "tp"), None, None, None),
        P(),
        P("rep"),
        P(("rep", "dp"), None),
        P(("rep", "dp"), "tp", None),
    )
    out_specs = P(("rep", "dp"), "tp")
    return jax.shard_map(
        on_device, mesh=mesh, in_specs=in_specs, out_specs=out_specs, check_vma=False
    )
```

profile of v0, /device:TPU:0, one launch (start us, length us, event | category | flops | bytes accessed | tf_op | source)
XLA Modules:
  0.0 317.3 jit_solution(2541749351426581833)
XLA Ops:
  6.5 0.8 convert_element_type.54
  7.3 1.0 fusion.24
  8.4 0.9 fusion.60
  9.3 2.0 all-gather
  11.4 0.9 select_reduce_fusion
  12.2 0.3 fusion.17
  12.5 0.1 fusion.48
  12.6 0.8 slice_bitcast_fusion.2
  13.4 0.1 convolution_bitcast_fusion.2
  13.5 0.1 convolution_bitcast_fusion.3
  13.7 1.1 convolution_bitcast_fusion.1
  14.8 0.8 pad_maximum_fusion
  15.7 0.9 fusion.26
  16.6 5.7 %fusion.47 = (bf16[4,512,8,128]{3,2,1,0:T(8,128)(2,1)}, bf16[4,512,8,128]{3,2,1,0:T(8,128)(2,1)}) fusion(bf16[4,512,8,256]{3,2,1,0:T(8,128)(2,1)} %bitcast.131), kind=kLoop, calls=%fused_computation.86 | loop fusion | bytes 16777216 | tf_op jit(solution)/shard_map/slice | solution.py:149
  22.4 2.9 fusion.33
  25.3 0.6 dynamic-slice
  25.9 38.7 %psum.7 = f32[4,2048]{1,0:T(4,128)S(1)} all-reduce(f32[4,2048]{1,0:T(4,128)S(1)} %fusion.33), channel_id=1, replica_groups=mesh['rep'=2,'dp'=2,'tp'=8] {'tp'}, use_global_device_ids=true, to_apply=%region_7.8 | all-reduce | flops 8192 | bytes 65536 | tf_op jit(solution)/shard_map/psum | solution.py:128
  64.7 42.2 %all-reduce.3.cloned.1.call-done = f32[16,4,1280]{2,1,0:T(4,128)} async-done(((f32[16,4,1280]{2,1,0:T(4,128)}), f32[16,4,1280]{2,1,0:T(4,128)}) %all-reduce.3.cloned.1.call-update) | async-done | bytes 327696
  106.9 1.4 dynamic-slice_bitcast_fusion
  108.2 8.2 %fusion.16 = f32[1,4,8,128]{3,1,2,0:T(4,128)S(1)} fusion(bf16[4,8192]{1,0:T(4,128)(2,1)S(1)} %fusion.26, bf16[8192,1024]{1,0:T(8,128)(2,1)} %param.16, f32[4,1280]{1,0:T(4,128)S(1)} %dynamic-slice_bitcast_fusion), kind=kOutput, calls=%fused_computation.20 | convolution fusion | flops 67112960 | bytes 16875520 | tf_op jit(solution)/shard_map/dot_general | solution.py:132
  116.5 0.1 subtract_convert_fusion
  116.6 0.1 multiply_subtract_fusion
  116.6 0.1 fusion.59
  116.7 31.7 %all_gather.16 = bf16[4,8192]{1,0:T(4,128)(2,1)S(1)} all-gather(bf16[4,1024]{1,0:T(4,128)(2,1)S(1)} %bitcast.136), channel_id=1, replica_groups=mesh['rep'=2,'dp'=2,'tp'=8] {'tp'}, dimensions={1}, use_global_device_ids=true | all-gather | bytes 73728 | tf_op jit(solution)/shard_map/all_gather | solution.py:145
  148.4 1.3 fusion.49
  149.7 1.5 fusion.13
  151.3 0.1 all_gather_reshape.9
  151.4 0.2 fusion.19
  151.6 0.1 all_gather_reshape.10
  151.7 26.0 %all_gather.18 = f32[8,4,64]{2,1,0:T(4,128)S(1)} all-gather(f32[1,4,64]{2,1,0:T(4,128)S(1)} %all_gather_reshape.10), channel_id=1, replica_groups=mesh['rep'=2,'dp'=2,'tp'=8] {'tp'}, dimensions={0}, use_global_device_ids=true | all-gather | bytes 9216 | tf_op jit(solution)/shard_map/all_gather | solution.py:18
  177.7 26.1 %all_gather.17 = f32[8,4,64]{2,1,0:T(4,128)S(1)} all-gather(f32[1,4,64]{2,1,0:T(4,128)S(1)} %all_gather_reshape.9), channel_id=1, replica_groups=mesh['rep'=2,'dp'=2,'tp'=8] {'tp'}, dimensions={0}, use_global_device_ids=true | all-gather | bytes 9216 | tf_op jit(solution)/shard_map/all_gather | solution.py:18
  203.9 0.2 fusion.39
  204.1 0.9 slice_bitcast_fusion
  205.0 7.8 %while.19 = (s32[]{:T(128)}, f32[4,64]{1,0:T(4,128)S(1)}, f32[4,64]{1,0:T(4,128)S(1)}, f32[4,64,128]{2,1,0:T(8,128)S(1)}, f32[8,4,64]{2,1,0:T(4,128)S(1)}, /*ind...) while((s32[]{:T(128)}, f32[4,64]{1,0:T(4,128)S(1)}, ...), condition=%wide.region_6.7_spmd, body=%wide.region_5.6_spmd.sunk | while | flops 99845 | bytes 403607 | solution.py:23
  205.0 1.1 fusion.64
  206.2 1.1 fusion.64
  207.3 1.1 fusion.64
  208.4 1.1 fusion.64
  209.5 1.1 fusion.64
  210.6 1.1 fusion.64
  211.8 1.1 fusion.64
  212.8 0.1 multiply_add_fusion.1
  212.9 0.1 fusion.35
  213.0 8.0 %convolution_bitcast_fusion = f32[8192,4]{0,1:T(4,128)S(1)} fusion(bf16[1024,8192]{1,0:T(8,128)(2,1)} %param.18, bf16[1,4,8,128]{3,2,1,0:T(8,128)(2,1)S(1)} %fusion.35), kind=kOutput, calls=%fused_computation.8 | convolution fusion | flops 67108864 | bytes 16916480 | tf_op jit(solution)/shard_map/dot_general | solution.py:184
  221.1 2.6 copy.34
  223.7 85.2 %reduce-scatter.4.cloned.1.call-done = f32[1024,4]{1,0:T(8,128)} async-done(((f32[8192,4]{1,0:T(8,128)}), f32[1024,4]{1,0:T(8,128)}) %reduce-scatter.4.cloned.1.call-update) | async-done | bytes 16400
  308.9 1.1 convert_element_type.66
  310.0 0.7 copy.45
  (37 shorter events, 0.6 us)
Async XLA Ops:
  6.5 5.7 %copy-start = (bf16[1,48,8192]{2,1,0:T(8,128)(2,1)S(1)}, bf16[1,48,8192]{2,1,0:T(8,128)(2,1)}, u32[]{:S(2)}) copy-start(bf16[1,48,8192]{2,1,0:T(8,128)(2,1)} %param.19) | copy-start | bytes 2359300
  6.5 100.3 %all-reduce.3.cloned.1.call-start = ((), (), s32[]{:S(2)}) async-start(), calls=%async_computation.3 | async-start | bytes 655360
  15.6 188.4 %all-gather.3.cloned.1.call-start = ((), (), s32[]{:S(2)}) async-start(), calls=%async_computation.1 | async-start | bytes 1179648 | tf_op jit(solution)/shard_map/all_gather | solution.py:18
  16.6 5.7 %copy-start.3 = (s32[1,4]{1,0:T(1,128)S(1)}, s32[1,4]{1,0:T(1,128)}, u32[]{:S(2)}) copy-start(s32[1,4]{1,0:T(1,128)} %param.24) | copy-start | bytes 52
  22.4 3.0 copy-start.4
  108.2 40.2 %copy-start.2 = (bf16[4,512,8,128]{3,2,1,0:T(8,128)(2,1)S(1)}, bf16[4,512,8,128]{3,2,1,0:T(8,128)(2,1)}, u32[]{:S(2)}) copy-start(bf16[4,512,8,128]{3,2,1,0:T(8,128)(2,1)} %get-tuple-element.208) | copy-start | bytes 12582916
  116.4 33.3 %copy-start.1 = (bf16[4,512,8,128]{3,2,1,0:T(8,128)(2,1)S(1)}, bf16[4,512,8,128]{3,2,1,0:T(8,128)(2,1)}, u32[]{:S(2)}) copy-start(bf16[4,512,8,128]{3,2,1,0:T(8,128)(2,1)} %get-tuple-element.207) | copy-start | bytes 12582916
  151.3 157.7 %reduce-scatter.4.cloned.1.call-start = ((), (), s32[]{:S(2)}) async-start(), calls=%async_computation.2 | async-start | bytes 4718592
Sparse Core Ops, SparseCore 0:
  15.7 91.0 all-reduce.2
  151.4 40.1 all-gather.2
  223.8 85.0 reduce-scatter.3
where the time goes:
time: 318 us; the launch traced here: 317 us
  waiting for transfers between devices  127 us (40%)
  blocking collectives  125 us (39%)
  matrix products  23.8 us (7%)
  other arithmetic  15 us (5%)
  between operations  13.2 us (4%)
  local copies, waits for them, and re-layouts  13.1 us (4%)
    unnamed x5, waiting for transfers between devices  127 us
    all_gather x2, blocking collectives, combined_all(): gathered = jax.tree.map(lambda a: lax.all_gather(a, axis), part)  52.1 us
    psum x1, blocking collectives, on_device(): kv_sum = lax.psum(kv_part, 'tp')  38.7 us
    all_gather x1, blocking collectives, on_device(): lax.all_gather(query.reshape(requests, head_cols), 'tp', axis=1, tiled=True)  31.7 us
    dot_general x1, matrix products, on_device(): jnp.dot(normed, query_matrix, preferred_element_type=jnp.float32)  8.18 us
    dot_general x1, matrix products, on_device(): lax.dot_general(output_weight, attended, (((0,), (1,)), ((), ())), prefer...  8.05 us
    add x7, other arithmetic, combine_parts(): acc_early * factor_early[..., None] + acc_late * factor_late[..., None]  7.5 us
  transfers between devices with their start and end apart: 3, of which 2 were waited for; matrix products, arithmetic and copies ran while one was open for 3% of the time, Pallas kernels for 0%

commit v1 on v0

--- a/solution.py
+++ b/solution.py
@@ -1,6 +1,11 @@
+import functools
+
 import jax
 import jax.numpy as jnp
+import numpy as np
 from jax import lax
+from jax.experimental import pallas as pl
+from jax.experimental.pallas import tpu as pltpu
 from jax.sharding import PartitionSpec as P
 
 QUERY_HEADS = 64
@@ -191,6 +196,425 @@
     return shares.T.astype(jnp.bfloat16)
 
 
+MESH = pl.DeviceIdType.MESH
+
+
+def attention_kernel(
+    n,
+    table_ref,
+    tenant_ref,
+    length_ref,
+    tokens_ref,
+    gain_ref,
+    freq_ref,
+    query_hbm,
+    kv_hbm,
+    output_hbm,
+    down_hbm,
+    up_query_hbm,
+    up_kv_hbm,
+    cache_hbm,
+    out_ref,
+    wq,
+    wkv,
+    wo,
+    cache,
+    down,
+    up_query,
+    up_kv,
+    normed_chunks,
+    cos_ref,
+    sin_ref,
+    rows_ref,
+    value_ref,
+    term_send,
+    term_recv,
+    all_queries,
+    score_ref,
+    part_send,
+    part_recv,
+    flat_ref,
+    share_send,
+    share_recv,
+    wq_sem,
+    kv_sem,
+    wo_sem,
+    cache_sem,
+    own_sem,
+    adapter_send,
+    adapter_recv,
+    send_sem,
+    recv_sem,
+):
+    me = lax.axis_index("tp")
+    core = lax.axis_index("dp")
+    reqs = tokens_ref.shape[0]
+    chunks = wq.shape[0]
+    depth = wq.shape[1]
+    cols = wq.shape[2]
+    width = normed_chunks.shape[0] * normed_chunks.shape[2]
+    span = cache.shape[1]
+    heads = cols // HEAD_SIZE
+    factor = HEAD_SIZE ** (-0.5)
+
+    own_adapter = [
+        pltpu.make_async_copy(down_hbm.at[0], down.at[0], own_sem.at[0]),
+        pltpu.make_async_copy(up_query_hbm.at[0], up_query.at[0], own_sem.at[1]),
+        pltpu.make_async_copy(up_kv_hbm.at[0], up_kv.at[0], own_sem.at[2]),
+    ]
+    kv_copy = pltpu.make_async_copy(kv_hbm, wkv, kv_sem)
+    wq_copy = [
+        pltpu.make_async_copy(query_hbm.at[pl.ds(c * depth, depth)], wq.at[c], wq_sem.at[c])
+        for c in range(chunks)
+    ]
+    cache_copy = [
+        pltpu.make_async_copy(cache_hbm.at[r], cache.at[r], cache_sem.at[r]) for r in range(reqs)
+    ]
+    wo_copy = [
+        pltpu.make_async_copy(output_hbm.at[:, pl.ds(c * cols, cols)], wo.at[c], wo_sem.at[c])
+        for c in range(n)
+    ]
+
+    def peer(k):
+        return lax.rem(me + k, n)
+
+    barrier = pltpu.get_barrier_semaphore()
+    pl.semaphore_signal(barrier, inc=1, device_id={"dp": 1 - core}, device_id_type=MESH)
+    for k in range(1, n):
+        pl.semaphore_signal(barrier, inc=1, device_id={"tp": peer(k)}, device_id_type=MESH)
+    for copy in own_adapter + [kv_copy] + wq_copy + cache_copy + wo_copy:
+        copy.start()
+
+    wide = tokens_ref[...].astype(jnp.float32)
+    inverse = lax.rsqrt(jnp.sum(wide * wide, axis=1, keepdims=True) / width + norm_eps)
+    normed = (wide * inverse * gain_ref[...].astype(jnp.float32)).astype(jnp.bfloat16)
+    for c in range(chunks):
+        normed_chunks[c] = normed[:, c * depth : (c + 1) * depth]
+
+    table_rows = rows_ref.shape[0]
+    row = lax.broadcasted_iota(jnp.int32, (table_rows, HEAD_SIZE), 0)
+    lane_t = lax.broadcasted_iota(jnp.int32, (table_rows, HEAD_SIZE), 1)
+    request = jnp.where(row < reqs * heads, row // heads, row - reqs * heads)
+    place = jnp.zeros((table_rows, HEAD_SIZE), jnp.int32)
+    for r in range(reqs):
+        place = jnp.where(request == r, length_ref[0, r], place)
+    angle = place.astype(jnp.float32) * freq_ref[...]
+    cos_ref[...] = jnp.cos(angle)
+    sin_ref[...] = jnp.where(lane_t < HEAD_SIZE // 2, -1.0, 1.0) * jnp.sin(angle)
+    rows_ref[...] = jnp.zeros_like(rows_ref)
+
+    pl.semaphore_wait(barrier, n)
+
+    adapter = [
+        pltpu.make_async_remote_copy(
+            src_ref=source,
+            dst_ref=target,
+            send_sem=adapter_send.at[i],
+            recv_sem=adapter_recv.at[i],
+            device_id={"dp": 1 - core},
+            device_id_type=MESH,
+        )
+        for i, (source, target) in enumerate(
+            (
+                (down_hbm.at[0], down.at[1]),
+                (up_query_hbm.at[0], up_query.at[1]),
+                (up_kv_hbm.at[0], up_kv.at[1]),
+            )
+        )
+    ]
+    for copy in adapter:
+        copy.start()
+
+    kv_copy.wait()
+    kv_part = jnp.dot(normed_chunks[me], wkv[...], preferred_element_type=jnp.float32)
+    for copy in own_adapter:
+        copy.wait()
+    for copy in adapter:
+        copy.wait()
+    which = lax.broadcasted_iota(jnp.int32, (reqs, 3 * ADAPTER_RANK), 0)
+    slots = jnp.zeros((reqs, 3 * ADAPTER_RANK), jnp.int32)
+    for r in range(reqs):
+        slots = jnp.where(which == r, table_ref[tenant_ref[core * reqs + r]], slots)
+    rank_rows = []
+    for a in range(2):
+        device = jnp.where(a == 0, core, 1 - core) * n + me
+        full = lax.dot_general(
+            normed, down[a], (((1,), (1,)), ((), ())), preferred_element_type=jnp.float32
+        )
+        rank_rows.append(jnp.where(slots == device, full, 0.0).astype(jnp.bfloat16))
+    kv_terms = []
+    for i in range(2):
+        first = (i + 1) * ADAPTER_RANK
+        term = kv_part[:, i * KEY_VALUE_HEADS * HEAD_SIZE : (i + 1) * KEY_VALUE_HEADS * HEAD_SIZE]
+        for a in range(2):
+            term = term + jnp.dot(
+                rank_rows[a][:, first : first + ADAPTER_RANK],
+                up_kv[a, i],
+                preferred_element_type=jnp.float32,
+            )
+        kv_terms.append(term)
+    for p in range(n):
+        term = sum(
+            jnp.dot(
+                rank_rows[a][:, :ADAPTER_RANK],
+                up_query[a, :, p * cols : (p + 1) * cols],
+                preferred_element_type=jnp.float32,
+            )
+            for a in range(2)
+        )
+        term_send[p, :, :cols] = term
+        for i in range(2):
+            term_send[p, :, cols + i * HEAD_SIZE : cols + (i + 1) * HEAD_SIZE] = kv_terms[i][
+                :, p * HEAD_SIZE : (p + 1) * HEAD_SIZE
+            ]
+
+    def sends(phase, source, target):
+        return [
+            pltpu.make_async_remote_copy(
+                src_ref=source(k),
+                dst_ref=target(k),
+                send_sem=send_sem.at[phase, k],
+                recv_sem=recv_sem.at[phase, k],
+                device_id={"tp": peer(k)},
+                device_id_type=MESH,
+            )
+            for k in range(1, n)
+        ]
+
+    term_copy = sends(0, lambda k: term_send.at[peer(k)], lambda k: term_recv.at[k])
+    for copy in term_copy:
+        copy.start()
+
+    query_raw = jnp.zeros((reqs, cols), jnp.float32)
+    for c in range(chunks):
+        wq_copy[c].wait()
+        query_raw = query_raw + jnp.dot(
+            normed_chunks[c], wq[c], preferred_element_type=jnp.float32
+        )
+    for copy in term_copy:
+        copy.wait_recv()
+    received = term_send[me]
+    for k in range(1, n):
+        received = received + term_recv[k]
+    query_raw = query_raw + received[:, :cols]
+    for r in range(reqs):
+        for h in range(heads):
+            rows_ref[r * heads + h : r * heads + h + 1, :] = query_raw[
+                r : r + 1, h * HEAD_SIZE : (h + 1) * HEAD_SIZE
+            ]
+    rows_ref[reqs * heads : reqs * heads + reqs, :] = received[:, cols : cols + HEAD_SIZE]
+    value_ref[...] = received[:, cols + HEAD_SIZE :].astype(jnp.bfloat16).astype(jnp.float32)
+    plain = rows_ref[...]
+    rotated = plain * cos_ref[...] + pltpu.roll(plain, HEAD_SIZE // 2, 1) * sin_ref[...]
+    rotated = rotated.astype(jnp.bfloat16)
+    all_queries[me] = rotated[: reqs * heads]
+    query_copy = sends(1, lambda k: all_queries.at[me], lambda k: all_queries.at[me])
+    for copy in query_copy:
+        copy.start()
+    rounded = rotated.astype(jnp.float32)
+    own_scores = []
+    for r in range(reqs):
+        key_row = rounded[reqs * heads + r : reqs * heads + r + 1]
+        own_scores.append(
+            jnp.sum(rounded[r * heads : (r + 1) * heads] * key_row, axis=1, keepdims=True) * factor
+        )
+    for copy in query_copy:
+        copy.wait_recv()
+
+    groups = KEY_VALUE_HEADS
+    grouped = all_queries[...].astype(jnp.float32)
+    piece = 512
+    pieces = span // piece
+    lane = lax.broadcasted_iota(jnp.int32, (heads, piece), 1)
+    lane_tile = lax.broadcasted_iota(jnp.int32, (heads, HEAD_SIZE), 1)
+    marks = jnp.zeros((heads, HEAD_SIZE), jnp.float32)
+    for r in range(reqs):
+        cache_copy[r].wait()
+        limit = length_ref[0, r] - me * (span // groups)
+        query_r = grouped[:, r * heads : (r + 1) * heads, :].reshape(n * heads, HEAD_SIZE)
+        query_r = query_r.astype(jnp.bfloat16)
+        top = jnp.full((heads, HEAD_SIZE), neutral, jnp.float32)
+        for c in range(pieces):
+            dots = lax.dot_general(
+                query_r,
+                cache[r, c * piece : (c + 1) * piece, :HEAD_SIZE],
+                (((1,), (1,)), ((), ())),
+                preferred_element_type=jnp.float32,
+            )
+            scores = dots[:heads]
+            for g in range(1, groups):
+                scores = jnp.where(
+                    lane % groups == g, dots[g * heads : (g + 1) * heads], scores
+                )
+            usable = (lane + c * piece) // groups < limit
+            scores = jnp.where(usable, scores * factor, neutral)
+            score_ref[:, c * piece : (c + 1) * piece] = scores
+            for i in range(piece // HEAD_SIZE):
+                top = jnp.maximum(top, scores[:, i * HEAD_SIZE : (i + 1) * HEAD_SIZE])
+        shift = groups
+        while shift < HEAD_SIZE:
+            top = jnp.maximum(top, pltpu.roll(top, shift, 1))
+            shift *= 2
+        top_wide = jnp.concatenate([top] * (piece // HEAD_SIZE), axis=1)
+        total = jnp.zeros((heads, HEAD_SIZE), jnp.float32)
+        acc = jnp.zeros((n * heads, HEAD_SIZE), jnp.float32)
+        for c in range(pieces):
+            usable = (lane + c * piece) // groups < limit
+            weights = jnp.where(
+                usable, jnp.exp(score_ref[:, c * piece : (c + 1) * piece] - top_wide), 0.0
+            )
+            for i in range(piece // HEAD_SIZE):
+                total = total + weights[:, i * HEAD_SIZE : (i + 1) * HEAD_SIZE]
+            spread = jnp.concatenate(
+                [jnp.where(lane % groups == g, weights, 0.0) for g in range(groups)], axis=0
+            ).astype(jnp.bfloat16)
+            acc = acc + jnp.dot(
+                spread,
+                cache[r, c * piece : (c + 1) * piece, HEAD_SIZE:],
+                preferred_element_type=jnp.float32,
+            )
+        shift = groups
+        while shift < HEAD_SIZE:
+            total = total + pltpu.roll(total, shift, 1)
+            shift *= 2
+        marks = jnp.where(lane_tile // groups == r, top, marks)
+        marks = jnp.where(lane_tile // groups == reqs + r, total, marks)
+        for g in range(groups):
+            part_send[g, r] = acc[g * heads : (g + 1) * heads]
+    for g in range(groups):
+        part_send[g, reqs] = marks
+    part_copy = sends(2, lambda k: part_send.at[peer(k)], lambda k: part_recv.at[k])
+    for copy in part_copy:
+        copy.start()
+    part_recv[0] = part_send[me]
+    for copy in part_copy:
+        copy.wait_recv()
+
+    tiles = [part_recv[k, reqs] for k in range(n)]
+    highest = functools.reduce(jnp.maximum, tiles)
+    scales = [jnp.exp(tile - highest) for tile in tiles]
+    totals = sum(
+        scale * pltpu.roll(tile, HEAD_SIZE - reqs * groups, 1)
+        for scale, tile in zip(scales, tiles)
+    )
+    for r in range(reqs):
+        chosen = lane_tile == r * groups + me
+
+        def pick(tile):
+            return jnp.sum(jnp.where(chosen, tile, 0.0), axis=1, keepdims=True)
+
+        merged = sum(pick(scales[k]) * part_recv[k, r] for k in range(n))
+        merged_top = pick(highest)
+        top_all = jnp.maximum(merged_top, own_scores[r])
+        old = jnp.exp(merged_top - top_all)
+        new = jnp.exp(own_scores[r] - top_all)
+        attended = (merged * old + new * value_ref[r : r + 1, :]) / (pick(totals) * old + new)
+        for h in range(heads):
+            flat_ref[r : r + 1, h * HEAD_SIZE : (h + 1) * HEAD_SIZE] = attended[h : h + 1]
+    attended = flat_ref[...].astype(jnp.bfloat16)
+
+    for copy in wo_copy:
+        copy.wait()
+    share_copy = sends(3, lambda k: share_send.at[peer(k)], lambda k: share_recv.at[k])
+    for k in range(1, n):
+        share_send[peer(k)] = jnp.dot(
+            attended, wo[peer(k)], preferred_element_type=jnp.float32
+        )
+        share_copy[k - 1].start()
+    mixed = jnp.dot(attended, wo[me], preferred_element_type=jnp.float32)
+    for k in range(1, n):
+        share_copy[k - 1].wait_recv()
+        mixed = mixed + share_recv[k]
+    out_ref[...] = mixed
+    for copy in term_copy + query_copy + part_copy + share_copy:
+        copy.wait_send()
+
+
+def on_device_fused(
+    tokens,
+    gain,
+    query_matrix,
+    key_value_weight,
+    output_weight,
+    adapter_down_factors,
+    adapter_up_query,
+    adapter_up_key_value,
+    tenant_slot_table,
+    request_tenant_index,
+    lengths,
+    cache,
+):
+    n = lax.axis_size("tp")
+    reqs, width = tokens.shape
+    cols = query_matrix.shape[1]
+    heads = cols // HEAD_SIZE
+    rows = -(-(reqs * heads + reqs) // 8) * 8
+    half = HEAD_SIZE // 2
+    power = np.arange(HEAD_SIZE) % half * 2.0 / HEAD_SIZE
+    frequency = jnp.asarray((theta_base ** -power).astype(np.float32)[None, :])
+    smem = pl.BlockSpec(memory_space=pltpu.SMEM)
+    vmem = pl.BlockSpec(memory_space=pltpu.VMEM)
+    hbm = pl.BlockSpec(memory_space=pl.ANY)
+    bf16, f32 = jnp.bfloat16, jnp.float32
+    dma = pltpu.SemaphoreType.DMA
+    share = pl.pallas_call(
+        functools.partial(attention_kernel, n),
+        out_shape=jax.ShapeDtypeStruct((reqs, cols), f32),
+        in_specs=[smem] * 3 + [vmem] * 3 + [hbm] * 7,
+        out_specs=vmem,
+        scratch_shapes=[
+            pltpu.VMEM((n, width // n, cols), bf16),
+            pltpu.VMEM(key_value_weight.shape, bf16),
+            pltpu.VMEM((n, output_weight.shape[0], width // n), bf16),
+            pltpu.VMEM(cache.shape, bf16),
+            pltpu.VMEM((2,) + adapter_down_factors.shape[1:], bf16),
+            pltpu.VMEM((2,) + adapter_up_query.shape[1:], bf16),
+            pltpu.VMEM((2,) + adapter_up_key_value.shape[1:], bf16),
+            pltpu.VMEM((n, reqs, width // n), bf16),
+            pltpu.VMEM((rows, HEAD_SIZE), f32),
+            pltpu.VMEM((rows, HEAD_SIZE), f32),
+            pltpu.VMEM((rows, HEAD_SIZE), f32),
+            pltpu.VMEM((reqs, HEAD_SIZE), f32),
+            pltpu.VMEM((n, reqs, cols + 2 * HEAD_SIZE), f32),
+            pltpu.VMEM((n, reqs, cols + 2 * HEAD_SIZE), f32),
+            pltpu.VMEM((n, reqs * heads, HEAD_SIZE), bf16),
+            pltpu.VMEM((heads, cache.shape[1]), f32),
+            pltpu.VMEM((n, reqs + 1, heads, HEAD_SIZE), f32),
+            pltpu.VMEM((n, reqs + 1, heads, HEAD_SIZE), f32),
+            pltpu.VMEM((reqs, cols), f32),
+            pltpu.VMEM((n, reqs, width // n), f32),
+            pltpu.VMEM((n, reqs, width // n), f32),
+            dma((n,)),
+            dma,
+            dma((n,)),
+            dma((reqs,)),
+            dma((3,)),
+            dma((3,)),
+            dma((3,)),
+            dma((4, n)),
+            dma((4, n)),
+        ],
+        compiler_params=pltpu.CompilerParams(
+            collective_id=0, has_side_effects=True, vmem_limit_bytes=60 * 2**20
+        ),
+    )(
+        tenant_slot_table,
+        request_tenant_index,
+        lengths,
+        tokens,
+        gain.reshape(1, width),
+        frequency,
+        query_matrix,
+        key_value_weight,
+        output_weight,
+        adapter_down_factors,
+        adapter_up_query,
+        adapter_up_key_value,
+        cache,
+    )
+    return share.astype(bf16)
+
+
 def solution(mesh):
     in_specs = (
         P(("rep", "dp"), None),
@@ -207,6 +631,8 @@
         P(("rep", "dp"), "tp", None),
     )
     out_specs = P(("rep", "dp"), "tp")
+    fused = mesh.shape["tp"] == KEY_VALUE_HEADS and mesh.shape["dp"] == 2
+    body = on_device_fused if fused else on_device
     return jax.shard_map(
-        on_device, mesh=mesh, in_specs=in_specs, out_specs=out_specs, check_vma=False
-    )
+        body, mesh=mesh, in_specs=in_specs, out_specs=out_specs, check_vma=False
+    )

time: 318 us -> 46.8 us (0.15)
  waiting for transfers between devices: 127 us -> 0 us
  blocking collectives: 125 us -> 0 us
  Pallas kernels: 0 us -> 43.9 us
  matrix products: 23.8 us -> 0 us
  other arithmetic: 15 us -> 1.32 us
  between operations: 13.2 us -> 0.01 us
  local copies, waits for them, and re-layouts: 13.1 us -> 1.34 us
    unnamed x5 -> x0, waiting for transfers between devices: 127 us -> none
    all_gather x4 -> x0, blocking collectives: 85.8 us -> none  [the longest x2 52.1 us: combined_all(): gathered = jax.tree.map(lambda a: lax.all_gather(a, axis), part)]
    pallas_call x0 -> x1, Pallas kernels: none -> 43.9 us  [on_device_fused(): pl.pallas_call(functools.partial(attention_kernel, n), out_shape=jax.Shap...]
    psum x1 -> x0, blocking collectives: 38.7 us -> none  [on_device(): kv_sum = lax.psum(kv_part, 'tp')]
    dot_general x10 -> x0, matrix products: 23.8 us -> none  [the longest x1 8.18 us: on_device(): jnp.dot(normed, query_matrix, preferred_element_type=jnp.float32)]
    add x16 -> x0, other arithmetic: 7.77 us -> none  [the longest x7 7.5 us: combine_parts(): acc_early * factor_early[..., None] + acc_late * factor_late[..., None]]
    slice x2 -> x0, local copies, waits for them, and re-layouts: 5.8 us -> none  [the longest x1 5.72 us: on_device(): cached_values = local_rows[..., HEAD_SIZE:]]
    unnamed x17 -> x0, local copies, waits for them, and re-layouts: 4.81 us -> none
  transfers between devices with their start and end apart: 3 -> 0, of which waited for: 2 -> 0; matrix products, arithmetic and copies ran while one was open for 3% -> 0% of each run, Pallas kernels for 0% -> 0%
where the time goes in v1:
time: 46.8 us; the launch traced here: 46.5 us
  Pallas kernels  43.9 us (94%)
  local copies, waits for them, and re-layouts  1.34 us (3%)
  other arithmetic  1.32 us (3%)
    pallas_call x1, Pallas kernels, on_device_fused(): pl.pallas_call(functools.partial(attention_kernel, n), out_shape=jax.Shap...  43.9 us
    reshape x1, local copies, waits for them, and re-layouts, on_device_fused(): gain.reshape(1, width)  1.34 us
    convert_element_type x1, other arithmetic, on_device_fused(): return share.astype(bf16)  1.32 us

profile of v1, /device:TPU:0, one launch (start us, length us, event | category | flops | bytes accessed | tf_op | source)
XLA Modules:
  0.0 46.5 jit_solution(8035307585260516090)
XLA Ops:
  0.0 1.3 %reshape.3.gain_ref = bf16[1,8192]{1,0:T(2,128)(2,1)} reshape(bf16[8192]{0:T(1024)(128)(2,1)} %param.14) | data formatting | bytes 32768 | tf_op jit(solution)/shard_map/reshape | solution.py:605
  1.3 43.9 %shard_map.127 = f32[4,1024]{1,0:T(4,128)} custom-call(s32[16]{0:T(128)} %table_ref.1, s32[8]{0:T(128)} %tenant_ref.1, s32[1,4]{1,0:T(1,128)} %length_ref.1, bf16[4,8192]{1,0:T(4,128)(2,1)} %tokens_ref.1, bf16[1,8192]{1,0:T(2,128)(2,1)} %reshape.3.gain_ref, f32[1,128]{1,0:T(1,128)} %constant.2.clone.freq_ref, bf16[8192,1024]{1,0:T(8,128)(2,1)} %query_hbm.1, ...), custom_call_target="tpu_custom_call" | custom-call | tf_op jit(solution)/shard_map/pallas_call | solution.py:560
  45.2 1.3 %convert_element_type.3 = bf16[4,1024]{1,0:T(4,128)(2,1)} convert(f32[4,1024]{1,0:T(4,128)} %shard_map.127) | non-fusion elementwise | flops 4096 | bytes 24576 | tf_op jit(solution)/shard_map/convert_element_type | solution.py:615

commit v2 on v1

--- a/solution.py
+++ b/solution.py
@@ -256,11 +256,12 @@
     span = cache.shape[1]
     heads = cols // HEAD_SIZE
     factor = HEAD_SIZE ** (-0.5)
+    ranks = 3 * ADAPTER_RANK
 
     own_adapter = [
-        pltpu.make_async_copy(down_hbm.at[0], down.at[0], own_sem.at[0]),
-        pltpu.make_async_copy(up_query_hbm.at[0], up_query.at[0], own_sem.at[1]),
-        pltpu.make_async_copy(up_kv_hbm.at[0], up_kv.at[0], own_sem.at[2]),
+        pltpu.make_async_copy(down_hbm.at[0], down.at[pl.ds(0, ranks)], own_sem.at[0]),
+        pltpu.make_async_copy(up_query_hbm.at[0], up_query.at[pl.ds(0, ADAPTER_RANK)], own_sem.at[1]),
+        pltpu.make_async_copy(up_kv_hbm.at[0], up_kv.at[:, pl.ds(0, ADAPTER_RANK)], own_sem.at[2]),
     ]
     kv_copy = pltpu.make_async_copy(kv_hbm, wkv, kv_sem)
     wq_copy = [
@@ -282,12 +283,12 @@
     pl.semaphore_signal(barrier, inc=1, device_id={"dp": 1 - core}, device_id_type=MESH)
     for k in range(1, n):
         pl.semaphore_signal(barrier, inc=1, device_id={"tp": peer(k)}, device_id_type=MESH)
-    for copy in own_adapter + [kv_copy] + wq_copy + cache_copy + wo_copy:
+    for copy in own_adapter + [kv_copy] + wq_copy:
         copy.start()
 
     wide = tokens_ref[...].astype(jnp.float32)
     inverse = lax.rsqrt(jnp.sum(wide * wide, axis=1, keepdims=True) / width + norm_eps)
-    normed = (wide * inverse * gain_ref[...].astype(jnp.float32)).astype(jnp.bfloat16)
+    normed = (wide * inverse * gain_ref[...].astype(jnp.float32).reshape(1, width)).astype(jnp.bfloat16)
     for c in range(chunks):
         normed_chunks[c] = normed[:, c * depth : (c + 1) * depth]
 
@@ -316,9 +317,9 @@
         )
         for i, (source, target) in enumerate(
             (
-                (down_hbm.at[0], down.at[1]),
-                (up_query_hbm.at[0], up_query.at[1]),
-                (up_kv_hbm.at[0], up_kv.at[1]),
+                (down_hbm.at[0], down.at[pl.ds(ranks, ranks)]),
+                (up_query_hbm.at[0], up_query.at[pl.ds(ADAPTER_RANK, ADAPTER_RANK)]),
+                (up_kv_hbm.at[0], up_kv.at[:, pl.ds(ADAPTER_RANK, ADAPTER_RANK)]),
             )
         )
     ]
@@ -326,43 +327,45 @@
         copy.start()
 
     kv_copy.wait()
+    for copy in cache_copy:
+        copy.start()
     kv_part = jnp.dot(normed_chunks[me], wkv[...], preferred_element_type=jnp.float32)
     for copy in own_adapter:
         copy.wait()
     for copy in adapter:
         copy.wait()
-    which = lax.broadcasted_iota(jnp.int32, (reqs, 3 * ADAPTER_RANK), 0)
-    slots = jnp.zeros((reqs, 3 * ADAPTER_RANK), jnp.int32)
+    which = lax.broadcasted_iota(jnp.int32, (reqs, 2 * ranks), 0)
+    slots = jnp.zeros((reqs, 2 * ranks), jnp.int32)
     for r in range(reqs):
         slots = jnp.where(which == r, table_ref[tenant_ref[core * reqs + r]], slots)
-    rank_rows = []
-    for a in range(2):
-        device = jnp.where(a == 0, core, 1 - core) * n + me
-        full = lax.dot_general(
-            normed, down[a], (((1,), (1,)), ((), ())), preferred_element_type=jnp.float32
-        )
-        rank_rows.append(jnp.where(slots == device, full, 0.0).astype(jnp.bfloat16))
+    owned = lax.broadcasted_iota(jnp.int32, (reqs, 2 * ranks), 1) < ranks
+    device = jnp.where(owned, core, 1 - core) * n + me
+    full = lax.dot_general(
+        normed, down[...], (((1,), (1,)), ((), ())), preferred_element_type=jnp.float32
+    )
+    rank_rows = jnp.where(slots == device, full, 0.0)
+
+    def rank_part(i):
+        first = i * ADAPTER_RANK
+        return jnp.concatenate(
+            [
+                rank_rows[:, first : first + ADAPTER_RANK],
+                rank_rows[:, ranks + first : ranks + first + ADAPTER_RANK],
+            ],
+            axis=1,
+        ).astype(jnp.bfloat16)
+
     kv_terms = []
     for i in range(2):
-        first = (i + 1) * ADAPTER_RANK
-        term = kv_part[:, i * KEY_VALUE_HEADS * HEAD_SIZE : (i + 1) * KEY_VALUE_HEADS * HEAD_SIZE]
-        for a in range(2):
-            term = term + jnp.dot(
-                rank_rows[a][:, first : first + ADAPTER_RANK],
-                up_kv[a, i],
-                preferred_element_type=jnp.float32,
-            )
-        kv_terms.append(term)
+        kv_terms.append(
+            kv_part[:, i * KEY_VALUE_HEADS * HEAD_SIZE : (i + 1) * KEY_VALUE_HEADS * HEAD_SIZE]
+            + jnp.dot(rank_part(i + 1), up_kv[i], preferred_element_type=jnp.float32)
+        )
+    query_rank = rank_part(0)
     for p in range(n):
-        term = sum(
-            jnp.dot(
-                rank_rows[a][:, :ADAPTER_RANK],
-                up_query[a, :, p * cols : (p + 1) * cols],
-                preferred_element_type=jnp.float32,
-            )
-            for a in range(2)
-        )
-        term_send[p, :, :cols] = term
+        term_send[p, :, :cols] = jnp.dot(
+            query_rank, up_query[:, p * cols : (p + 1) * cols], preferred_element_type=jnp.float32
+        )
         for i in range(2):
             term_send[p, :, cols + i * HEAD_SIZE : cols + (i + 1) * HEAD_SIZE] = kv_terms[i][
                 :, p * HEAD_SIZE : (p + 1) * HEAD_SIZE
@@ -383,6 +386,8 @@
 
     term_copy = sends(0, lambda k: term_send.at[peer(k)], lambda k: term_recv.at[k])
     for copy in term_copy:
+        copy.start()
+    for copy in wo_copy:
         copy.start()
 
     query_raw = jnp.zeros((reqs, cols), jnp.float32)
@@ -428,6 +433,15 @@
     lane = lax.broadcasted_iota(jnp.int32, (heads, piece), 1)
     lane_tile = lax.broadcasted_iota(jnp.int32, (heads, HEAD_SIZE), 1)
     marks = jnp.zeros((heads, HEAD_SIZE), jnp.float32)
+    first_half = reqs // 2
+
+    def part_sends(phase, first, count):
+        return sends(
+            phase,
+            lambda k: part_send.at[peer(k), pl.ds(first, count)],
+            lambda k: part_recv.at[k, pl.ds(first, count)],
+        )
+
     for r in range(reqs):
         cache_copy[r].wait()
         limit = length_ref[0, r] - me * (span // groups)
@@ -481,11 +495,16 @@
         marks = jnp.where(lane_tile // groups == reqs + r, total, marks)
         for g in range(groups):
             part_send[g, r] = acc[g * heads : (g + 1) * heads]
+        if r == first_half - 1:
+            early_copy = part_sends(2, 0, first_half)
+            for copy in early_copy:
+                copy.start()
     for g in range(groups):
         part_send[g, reqs] = marks
-    part_copy = sends(2, lambda k: part_send.at[peer(k)], lambda k: part_recv.at[k])
+    part_copy = part_sends(4, first_half, reqs + 1 - first_half)
     for copy in part_copy:
         copy.start()
+    part_copy = early_copy + part_copy
     part_recv[0] = part_send[me]
     for copy in part_copy:
         copy.wait_recv()
@@ -567,9 +586,9 @@
             pltpu.VMEM(key_value_weight.shape, bf16),
             pltpu.VMEM((n, output_weight.shape[0], width // n), bf16),
             pltpu.VMEM(cache.shape, bf16),
-            pltpu.VMEM((2,) + adapter_down_factors.shape[1:], bf16),
-            pltpu.VMEM((2,) + adapter_up_query.shape[1:], bf16),
-            pltpu.VMEM((2,) + adapter_up_key_value.shape[1:], bf16),
+            pltpu.VMEM((6 * ADAPTER_RANK, width), bf16),
+            pltpu.VMEM((2 * ADAPTER_RANK, adapter_up_query.shape[2]), bf16),
+            pltpu.VMEM((2, 2 * ADAPTER_RANK, adapter_up_key_value.shape[3]), bf16),
             pltpu.VMEM((n, reqs, width // n), bf16),
             pltpu.VMEM((rows, HEAD_SIZE), f32),
             pltpu.VMEM((rows, HEAD_SIZE), f32),
@@ -591,8 +610,8 @@
             dma((3,)),
             dma((3,)),
             dma((3,)),
-            dma((4, n)),
-            dma((4, n)),
+            dma((5, n)),
+            dma((5, n)),
         ],
         compiler_params=pltpu.CompilerParams(
             collective_id=0, has_side_effects=True, vmem_limit_bytes=60 * 2**20
@@ -602,7 +621,7 @@
         request_tenant_index,
         lengths,
         tokens,
-        gain.reshape(1, width),
+        gain,
         frequency,
         query_matrix,
         key_value_weight,

time: 46.8 us -> 39.5 us (0.84)
  Pallas kernels: 43.9 us -> 38 us
  local copies, waits for them, and re-layouts: 1.34 us -> 0 us
    pallas_call x1, Pallas kernels: 43.9 us -> 38 us  [on_device_fused(): pl.pallas_call(functools.partial(attention_kernel, n), out_shape=jax.Shap...]
    reshape x1 -> x0, local copies, waits for them, and re-layouts: 1.34 us -> none  [on_device_fused(): gain.reshape(1, width)]
where the time goes in v2:
time: 39.5 us; the launch traced here: 39.3 us
  Pallas kernels  38 us (96%)
  other arithmetic  1.32 us (3%)
    pallas_call x1, Pallas kernels, on_device_fused(): pl.pallas_call(functools.partial(attention_kernel, n), out_shape=jax.Shap...  38 us
    convert_element_type x1, other arithmetic, on_device_fused(): return share.astype(bf16)  1.32 us

profile of v2, /device:TPU:0, one launch (start us, length us, event | category | flops | bytes accessed | tf_op | source)
XLA Modules:
  0.0 39.3 jit_solution(1344634296573070693)
XLA Ops:
  0.0 38.0 %shard_map.127 = f32[4,1024]{1,0:T(4,128)} custom-call(s32[16]{0:T(128)} %table_ref.1, s32[8]{0:T(128)} %tenant_ref.1, s32[1,4]{1,0:T(1,128)} %length_ref.1, bf16[4,8192]{1,0:T(4,128)(2,1)} %tokens_ref.1, bf16[8192]{0:T(1024)(128)(2,1)} %gain_ref.1, f32[1,128]{1,0:T(1,128)} %constant.2.clone.freq_ref, bf16[8192,1024]{1,0:T(8,128)(2,1)} %query_hbm.1, ...), custom_call_target="tpu_custom_call" | custom-call | tf_op jit(solution)/shard_map/pallas_call | solution.py:579
  38.0 1.3 %convert_element_type.3 = bf16[4,1024]{1,0:T(4,128)(2,1)} convert(f32[4,1024]{1,0:T(4,128)} %shard_map.127) | non-fusion elementwise | flops 4096 | bytes 24576 | tf_op jit(solution)/shard_map/convert_element_type | solution.py:634
